TPU v7x, 256 devices: a whole 4x4x8 slice. The times are simulated.
256 devices in a mesh: dp: 16 (over z, x_hi), ctx: 16 (over x_lo, y, core).
Axes of the slice: x: 4 (x_hi: 2, x_lo: 2; x = x_hi * 2 + x_lo), y: 4, z: 8, core: 2. Of those that a mesh axis runs over, the one named last changes fastest.
Arguments:
- features: bfloat16 [16, 8192, 768], P('dp', 'ctx'), may hold values from -24 to 24
- bases: int32 [16, 8192], P('dp', 'ctx'), may hold values from 0 to 3
- dna_table: bfloat16 [4, 768], replicated, may hold values from -6 to 6
- norm_gain: bfloat16 [768], replicated, may hold values from 0.099609375 to 1.8984375
- w_conv: bfloat16 [5, 768, 768], replicated, may hold values from -0.09375 to 0.09375
- w_query: bfloat16 [768, 768], replicated, may hold values from -0.21875 to 0.21875
- w_key: bfloat16 [768, 768], replicated, may hold values from -0.21875 to 0.21875
- w_value: bfloat16 [768, 768], replicated, may hold values from -0.21875 to 0.21875
- w_out: bfloat16 [768, 768], replicated, may hold values from -0.21875 to 0.21875
- cotangent: bfloat16 [16, 512, 768], P('dp', 'ctx'), may hold values from -48 to 48
Outputs:
- grad_features: bfloat16 [16, 8192, 768], P('dp', 'ctx')
- grad_conv: float32 [768, 5, 768], P('ctx', None, 'dp')
All inputs are finite; a program needn't handle non-finite values.
Results may differ from a plain program's by a relative error of at most 0.025.
The roundings to bfloat16 on the way count: a program that leaves them out, or rounds other values in their place, can miss the bound.
Values may be sent and summed in bfloat16 or wider, within the bound.
A program may use at most 128 MiB of HBM per device.

v0:
```python
import jax
import jax.numpy as jnp
from jax import lax
from jax.sharding import PartitionSpec as P

HEADS = 6
DH = 128
EPSILON = 1e-06
GELU_SCALE = 0.7978845608028654
CUBIC = 0.044715


def extended(block, sides, width):
    for axis, dim in sides:
        count = lax.axis_size(axis)
        forward = [(i, i + 1) for i in range(count - 1)]
        backward = [(target, source) for source, target in forward]
        low = lax.ppermute(
            lax.slice_in_dim(block, block.shape[dim] - width, None, axis=dim), axis, forward
        )
        high = lax.ppermute(lax.slice_in_dim(block, 0, width, axis=dim), axis, backward)
        block = jnp.concatenate([low, block, high], axis=dim)
    return block


def gelu_pair(inputs):
    inner = GELU_SCALE * (inputs + CUBIC * inputs**3)
    tanh_val = jnp.tanh(inner)
    values = 0.5 * inputs * (1.0 + tanh_val)
    slopes = 0.5 * (1.0 + tanh_val) + 0.5 * inputs * (1.0 - tanh_val**2) * GELU_SCALE * (
        1.0 + 3.0 * CUBIC * inputs**2
    )
    return (values, slopes)


def heads_split(matrix):
    return matrix.reshape(matrix.shape[0], HEADS, DH)


def dot_right_t(left, right):
    return lax.dot_general(
        left, right, (((1,), (1,)), ((), ())), preferred_element_type=jnp.float32
    )


def dot_left_t(left, right):
    return lax.dot_general(
        left, right, (((0,), (0,)), ((), ())), preferred_element_type=jnp.float32
    )


def per_device(
    features, bases, dna_table, norm_gain, w_conv, w_query, w_key, w_value, w_out, cotangent
):
    seg_feat = features[0]
    seg_base = bases[0]
    seg_cot = cotangent[0]
    kernel = w_conv.shape[0]
    half_width = kernel // 2
    length = seg_feat.shape[0]
    channels = seg_feat.shape[1]
    tok_rows = seg_cot.shape[0]
    onehot = (seg_base[:, None] == jnp.arange(4, dtype=jnp.int32)[None, :]).astype(jnp.bfloat16)
    summed_in = seg_feat.astype(jnp.float32) + jnp.dot(
        onehot, dna_table, preferred_element_type=jnp.float32
    )
    inv_rms = lax.rsqrt(jnp.mean(summed_in * summed_in, axis=-1, keepdims=True) + EPSILON)
    normed = summed_in * inv_rms
    gain_f = norm_gain.astype(jnp.float32)
    pre_gelu = normed * gain_f
    gelu_val, slopes = gelu_pair(pre_gelu)
    act = gelu_val.astype(jnp.bfloat16)
    rimmed = extended(act[None], (("ctx", 1),), half_width)[0]
    conv = jnp.zeros((length, channels), jnp.float32)
    for offset in range(kernel):
        conv = conv + jnp.dot(
            rimmed[offset : offset + length], w_conv[offset], preferred_element_type=jnp.float32
        )
    resid = summed_in + conv
    pooled = resid.reshape(tok_rows, -1, channels).mean(axis=1).astype(jnp.bfloat16)
    queries = jnp.dot(pooled, w_query, preferred_element_type=jnp.float32).astype(jnp.bfloat16)
    keys_local = jnp.dot(pooled, w_key, preferred_element_type=jnp.float32).astype(jnp.bfloat16)
    values_local = jnp.dot(pooled, w_value, preferred_element_type=jnp.float32).astype(jnp.bfloat16)
    keys_all, values_all = (
        lax.all_gather(keys_local, "ctx", axis=0, tiled=True),
        lax.all_gather(values_local, "ctx", axis=0, tiled=True),
    )
    scale = 1.0 / DH**0.5
    query_heads = heads_split(queries)
    key_heads = heads_split(keys_all)
    value_heads = heads_split(values_all)
    scores = (
        jnp.einsum("qhd,khd->hqk", query_heads, key_heads, preferred_element_type=jnp.float32)
        * scale
    )
    row_max = jnp.max(scores, axis=-1, keepdims=True)
    expo = jnp.exp(scores - row_max)
    row_total = jnp.sum(expo, axis=-1, keepdims=True)
    probs = expo / row_total
    probs_b = probs.astype(jnp.bfloat16)
    attn_out = jnp.einsum("hqk,khd->qhd", probs_b, value_heads, preferred_element_type=jnp.float32)
    attn_out = attn_out.reshape(tok_rows, channels).astype(jnp.bfloat16)
    grad_attn = dot_right_t(seg_cot, w_out).astype(jnp.bfloat16)
    grad_heads = heads_split(grad_attn)
    grad_prob = jnp.einsum(
        "qhd,khd->hqk", grad_heads, value_heads, preferred_element_type=jnp.float32
    )
    delta_rows = jnp.sum(
        grad_heads.astype(jnp.float32) * heads_split(attn_out).astype(jnp.float32), axis=-1
    )
    row_delta = delta_rows.transpose(1, 0)[:, :, None]
    grad_score = (probs * (grad_prob - row_delta) * scale).astype(jnp.bfloat16)
    grad_q = jnp.einsum("hqk,khd->qhd", grad_score, key_heads, preferred_element_type=jnp.float32)
    grad_q = grad_q.reshape(tok_rows, channels).astype(jnp.bfloat16)
    term_k = jnp.einsum("hqk,qhd->khd", grad_score, query_heads, preferred_element_type=jnp.float32)
    term_v = jnp.einsum("hqk,qhd->khd", probs_b, grad_heads, preferred_element_type=jnp.float32)
    summed_kv = lax.psum_scatter(
        jnp.concatenate(
            (
                term_k.reshape(lax.axis_size("ctx") * tok_rows, channels),
                term_v.reshape(lax.axis_size("ctx") * tok_rows, channels),
            ),
            axis=1,
        ),
        "ctx",
        scatter_dimension=0,
        tiled=True,
    )
    grad_k = summed_kv[:, :channels].astype(jnp.bfloat16)
    grad_v = summed_kv[:, channels:].astype(jnp.bfloat16)
    grad_pooled = (
        seg_cot.astype(jnp.float32)
        + dot_right_t(grad_q, w_query)
        + dot_right_t(grad_k, w_key)
        + dot_right_t(grad_v, w_value)
    )
    pool_size = length // tok_rows
    grad_rows = jnp.repeat((grad_pooled / pool_size).astype(jnp.bfloat16), pool_size, axis=0)
    grad_pad = extended(grad_rows[None], (("ctx", 1),), half_width)[0]
    grad_act = jnp.zeros((length, channels), jnp.float32)
    for offset in range(kernel):
        begin = 2 * half_width - offset
        grad_act = grad_act + dot_right_t(grad_pad[begin : begin + length], w_conv[offset])
    windows = jnp.stack(
        [rimmed[offset : offset + length] for offset in range(kernel)], axis=2
    ).reshape(length, channels * kernel)
    factor = 1.0 / (lax.axis_size("dp") * length * lax.axis_size("ctx")) ** 0.5
    whole_terms = (dot_left_t(windows, grad_rows) * factor).reshape(channels, kernel, channels)
    shared = lax.psum_scatter(whole_terms, "ctx", scatter_dimension=0, tiled=True)
    grad_conv = lax.psum_scatter(shared, "dp", scatter_dimension=2, tiled=True)
    grad_norm = grad_act * slopes * gain_f
    grad_in = grad_rows.astype(jnp.float32) + inv_rms * (
        grad_norm - normed * jnp.mean(grad_norm * normed, axis=-1, keepdims=True)
    )
    return (grad_in.astype(jnp.bfloat16)[None], grad_conv)


def solution(mesh):
    in_specs = (
        P("dp", "ctx", None),
        P("dp", "ctx"),
        P(),
        P(),
        P(),
        P(),
        P(),
        P(),
        P(),
        P("dp", "ctx", None),
    )
    out_specs = (P("dp", "ctx", None), P("ctx", None, "dp"))
    return jax.shard_map(
        per_device, mesh=mesh, in_specs=in_specs, out_specs=out_specs, check_vma=False
    )
```

profile of v0, /device:TPU:8, one launch (start us, length us, event | category | flops | bytes accessed | tf_op | source)
XLA Modules:
  0.0 533.8 jit_solution(988875582411830763)
XLA Ops:
  8.0 1.7 multiply_reduce_fusion.1
  10.4 1.9 collective-permute-start
  12.3 3.9 collective-permute-start.1
  16.2 2.5 fusion.22
  18.8 1.1 fusion.40
  20.7 0.8 fusion.30
  22.3 1.1 bitcast_reduce_fusion
  23.4 0.9 fusion.39
  24.4 0.9 convolution_convert_fusion.2
  25.6 20.5 %all_gather.6 = bf16[512,768]{1,0:T(8,128)(2,1)} all-gather(bf16[32,768]{1,0:T(8,128)(2,1)S(1)} %convolution_convert_fusion.5), channel_id=1, replica_groups=mesh['dp'=16,'ctx'=16] {'ctx'}, dimensions={0}, use_global_device_ids=true | all-gather | bytes 835584 | tf_op jit(solution)/shard_map/all_gather | solution.py:85
  46.1 2.3 copy.36
  48.4 1.4 convolution_multiply_fusion.1
  50.6 0.9 fusion.100
  51.5 22.8 %all_gather.7 = bf16[512,768]{1,0:T(8,128)(2,1)} all-gather(bf16[32,768]{1,0:T(8,128)(2,1)S(1)} %copy-done.13), channel_id=1, replica_groups=mesh['dp'=16,'ctx'=16] {'ctx'}, dimensions={0}, use_global_device_ids=true | all-gather | bytes 835584 | tf_op jit(solution)/shard_map/all_gather | solution.py:86
  74.3 2.3 copy.39
  76.6 2.8 fusion.77
  79.5 2.4 fusion.38
  81.9 1.6 fusion.32
  84.6 2.0 pad_maximum_fusion
  86.6 3.6 copy.54
  90.9 1.1 bitcast_dynamic-update-slice_fusion.4
  91.9 1.1 bitcast_dynamic-update-slice_fusion.3
  93.0 1.6 bitcast_dynamic-update-slice_fusion.2
  94.6 1.2 bitcast_dynamic-update-slice_fusion.1
  95.8 1.1 bitcast_dynamic-update-slice_fusion
  96.8 8.4 %copy.48 = bf16[512,768,5]{0,2,1:T(8,128)(2,1)} copy(bf16[512,768,5]{1,0,2:T(8,128)(2,1)} %bitcast_dynamic-update-slice_fusion) | data formatting | bytes 7864320 | tf_op jit(solution)/shard_map/stack | solution.py:144
  105.3 8.5 %reshape.82 = bf16[512,3840]{0,1:T(8,128)(2,1)} reshape(bf16[512,768,5]{0,2,1:T(8,128)(2,1)} %copy.48) | data formatting | bytes 7864320 | tf_op jit(solution)/shard_map/reshape | solution.py:146
  113.8 1.3 fusion.41
  115.1 1.3 convolution_add_fusion.2
  116.4 38.6 %reduce-scatter.10.cloned.1.call-done = f32[32,1536]{1,0:T(8,128)} async-done(((f32[512,1536]{1,0:T(8,128)}), f32[32,1536]{1,0:T(8,128)}) %reduce-scatter.10.cloned.1.call-update) | async-done | bytes 196624
  155.0 1.1 copy.55
  156.1 1.7 convolution_add_fusion.1
  158.5 9.7 %convolution_multiply_fusion = f32[3840,768]{1,0:T(8,128)} fusion(bf16[512,3840]{0,1:T(8,128)(2,1)} %reshape.82, bf16[512,768]{1,0:T(8,128)(2,1)S(1)} %bitcast.148), kind=kOutput, calls=%fused_computation.1 | convolution fusion | flops 3022848000 | bytes 16515072 | tf_op jit(solution)/shard_map/dot_general | solution.py:47
  168.2 14.8 %reshape.83 = f32[768,5,768]{2,1,0:T(8,128)} reshape(f32[3840,768]{1,0:T(8,128)} %convolution_multiply_fusion) | data formatting | bytes 23592960 | tf_op jit(solution)/shard_map/reshape | solution.py:148
  183.1 2.4 collective-permute-start.2
  185.5 3.2 fusion.20
  188.8 2.1 collective-permute-start.3
  190.9 3.2 fusion.24
  194.2 99.7 %reduce-scatter.8.cloned.1.call-done = f32[48,5,768]{2,1,0:T(8,128)} async-done(((f32[768,5,768]{2,1,0:T(8,128)}), f32[48,5,768]{2,1,0:T(8,128)}) %reduce-scatter.8.cloned.1.call-update) | async-done | bytes 737296 | tf_op jit(solution)/shard_map/reduce_scatter | solution.py:149
  293.9 13.2 %copy.56 = f32[48,5,768]{1,0,2:T(8,128)} copy(f32[48,5,768]{2,1,0:T(8,128)} %reduce-scatter.8.cloned.1.call-done) | data formatting | bytes 1474560
  307.1 12.9 %reshape.87 = f32[768,240]{1,0:T(8,128)} reshape(f32[768,48,5]{2,1,0:T(8,128)} %bitcast.142) | data formatting | bytes 1474560
  319.9 2.1 fusion.28
  322.1 2.2 fusion.16
  324.3 3.3 multiply_reduce_fusion
  327.6 1.3 fusion.60
  328.9 195.8 %reduce-scatter.12.cloned.1.call-done = f32[48,240]{1,0:T(8,128)} async-done(((f32[768,240]{1,0:T(8,128)}), f32[48,240]{1,0:T(8,128)}) %reduce-scatter.12.cloned.1.call-update) | async-done | bytes 46096
  524.7 1.4 reshape.88
  526.1 1.2 copy.49
  (58 shorter events, 6.6 us)
Async XLA Ops:
  7.2 16.2 %copy-start = (bf16[768,768]{1,0:T(8,128)(2,1)S(1)}, bf16[768,768]{1,0:T(8,128)(2,1)}, u32[]{:S(2)}) copy-start(bf16[768,768]{1,0:T(8,128)(2,1)} %param.15) | copy-start | bytes 3538948
  7.2 147.8 %reduce-scatter.10.cloned.1.call-start = ((), (), s32[]{:S(2)}) async-start(), calls=%async_computation.4 | async-start | bytes 3342336
  10.4 9.5 %collective-permute-start = (bf16[1,2,768]{2,1,0:T(2,128)(2,1)S(1)}, bf16[1,2,768]{2,1,0:T(2,128)(2,1)S(1)}, u32[]{:S(2)}, u32[]{:S(2)}) collective-permute-start(bf16[1,2,768]{2,1,0:T(2,128)(2,1)S(1)} %get-tuple-element.8), channel_id=1, source_target_pairs={{0,1},{1,2},{2,3},{3,4},{4,5},{5,6},{6,7},{7,8},{8,9},{9,10},{10,1... | collective-permute-start | bytes 9224 | tf_op jit(solution)/shard_map/ppermute | solution.py:18
  12.3 6.4 %copy-start.8 = (bf16[768,768]{1,0:T(8,128)(2,1)S(1)}, bf16[768,768]{1,0:T(8,128)(2,1)}, u32[]{:S(2)}) copy-start(bf16[768,768]{1,0:T(8,128)(2,1)} %param.18) | copy-start | bytes 3538948
  12.3 6.4 %copy-start.12 = (bf16[1,32,768]{2,1,0:T(8,128)(2,1)S(1)}, bf16[1,32,768]{2,1,0:T(8,128)(2,1)}, u32[]{:S(2)}) copy-start(bf16[1,32,768]{2,1,0:T(8,128)(2,1)} %param.19) | copy-start | bytes 147460
  12.3 7.5 %copy-start.11 = (bf16[5,768,768]{2,1,0:T(8,128)(2,1)S(1)}, bf16[5,768,768]{2,1,0:T(8,128)(2,1)}, u32[]{:S(2)}) copy-start(bf16[5,768,768]{2,1,0:T(8,128)(2,1)} %param.14) | copy-start | bytes 17694724
  12.3 9.2 %collective-permute-start.1 = (bf16[1,2,768]{2,1,0:T(2,128)(2,1)S(1)}, bf16[1,2,768]{2,1,0:T(2,128)(2,1)S(1)}, u32[]{:S(2)}, u32[]{:S(2)}) collective-permute-start(bf16[1,2,768]{2,1,0:T(2,128)(2,1)S(1)} %get-tuple-element.9), channel_id=1, source_target_pairs={{1,0},{2,1},{3,2},{4,3},{5,4},{6,5},{7,6},{8,7},{9,8},{10,9},{11,1... | collective-permute-start | bytes 9224 | tf_op jit(solution)/shard_map/ppermute | solution.py:21
  19.9 0.8 copy-start.14
  22.3 2.1 copy-start.5
  23.4 1.9 copy-start.4
  48.4 3.1 copy-start.13
  49.8 0.8 copy-start.7
  81.9 2.3 copy-start.10
  81.9 2.7 copy-start.3
  83.5 0.7 copy-start.9
  90.2 0.7 copy-start.15
  90.2 203.6 %reduce-scatter.8.cloned.1.call-start = ((), (), s32[]{:S(2)}) async-start(), calls=%async_computation.3 | async-start | bytes 20054016 | tf_op jit(solution)/shard_map/reduce_scatter | solution.py:149
  105.3 8.5 %copy-start.2 = (bf16[512,768]{0,1:T(8,128)(2,1)S(1)}, bf16[512,768]{0,1:T(8,128)(2,1)}, u32[]{:S(2)}) copy-start(bf16[512,768]{0,1:T(8,128)(2,1)} %copy.36) | copy-start | bytes 2359300
  116.4 41.5 %copy-start.6 = (bf16[768,768]{1,0:T(8,128)(2,1)S(1)}, bf16[768,768]{1,0:T(8,128)(2,1)}, u32[]{:S(2)}) copy-start(bf16[768,768]{1,0:T(8,128)(2,1)} %param.17) | copy-start | bytes 3538948
  183.0 341.7 %reduce-scatter.12.cloned.1.call-start = ((), (), s32[]{:S(2)}) async-start(), calls=%async_computation.5 | async-start | bytes 835584
  183.1 7.8 %collective-permute-start.2 = (bf16[1,2,768]{2,1,0:T(2,128)(2,1)S(1)}, bf16[1,2,768]{2,1,0:T(2,128)(2,1)S(1)}, u32[]{:S(2)}, u32[]{:S(2)}) collective-permute-start(bf16[1,2,768]{2,1,0:T(2,128)(2,1)S(1)} %get-tuple-element.6), channel_id=1, source_target_pairs={{1,0},{2,1},{3,2},{4,3},{5,4},{6,5},{7,6},{8,7},{9,8},{10,9},{11,1... | collective-permute-start | bytes 9224 | tf_op jit(solution)/shard_map/ppermute | solution.py:21
  188.8 133.3 %collective-permute-start.3 = (bf16[1,2,768]{2,1,0:T(2,128)(2,1)S(1)}, bf16[1,2,768]{2,1,0:T(2,128)(2,1)S(1)}, u32[]{:S(2)}, u32[]{:S(2)}) collective-permute-start(bf16[1,2,768]{2,1,0:T(2,128)(2,1)S(1)} %get-tuple-element.7), channel_id=1, source_target_pairs={{0,1},{1,2},{2,3},{3,4},{4,5},{5,6},{6,7},{7,8},{8,9},{9,10},{10,1... | collective-permute-start | bytes 9224 | tf_op jit(solution)/shard_map/ppermute | solution.py:18
  322.0 2.3 copy-start.16
  322.0 2.3 copy-start.17
  327.6 199.7 %copy-start.1 = (bf16[768,768]{1,0:T(8,128)(2,1)S(1)}, bf16[768,768]{1,0:T(8,128)(2,1)}, u32[]{:S(2)}) copy-start(bf16[768,768]{1,0:T(8,128)(2,1)} %param.15) | copy-start | bytes 3538948
Sparse Core Ops, SparseCore 0:
  90.4 64.5 reduce-scatter.9
  183.2 110.6 reduce-scatter.7
  320.1 204.6 reduce-scatter.11
where the time goes:
time: 536 us; the launch traced here: 534 us
  waiting for transfers between devices  334 us (62%)
  local copies, waits for them, and re-layouts  71.8 us (13%)
  matrix products  48.2 us (9%)
  blocking collectives  43.3 us (8%)
  between operations  14.1 us (3%)
  other arithmetic  11.5 us (2%)
  starting transfers between devices  10.7 us (2%)
    unnamed x5, waiting for transfers between devices  234 us
    reduce_scatter x1, waiting for transfers between devices, per_device(): lax.psum_scatter(whole_terms, 'ctx', scatter_dimension=0, tiled=True)  99.7 us
    unnamed x42, local copies, waits for them, and re-layouts  35.3 us
    all_gather x1, blocking collectives, per_device(): lax.all_gather(values_local, 'ctx', axis=0, tiled=True)  22.8 us
    all_gather x1, blocking collectives, per_device(): lax.all_gather(keys_local, 'ctx', axis=0, tiled=True)  20.5 us
    dot_general x9, matrix products, dot_right_t(): lax.dot_general(left, right, (((1,), (1,)), ((), ())), preferred_element_...  18.7 us
    reshape x1, local copies, waits for them, and re-layouts, per_device(): (dot_left_t(windows, grad_rows) * factor).reshape(channels, kernel, chann...  14.8 us
  transfers between devices with their start and end apart: 7, of which 3 were waited for; matrix products, arithmetic and copies ran while one was open for 14% of the time, Pallas kernels for 0%

commit v1 on v0

--- a/solution.py
+++ b/solution.py
@@ -83,7 +83,9 @@
     values_local = jnp.dot(pooled, w_value, preferred_element_type=jnp.float32).astype(jnp.bfloat16)
     keys_all, values_all = (
         lax.all_gather(keys_local, "ctx", axis=0, tiled=True),
-        lax.all_gather(values_local, "ctx", axis=0, tiled=True),
+        jnp.concatenate(
+            lax.all_to_all(jnp.stack([values_local] * lax.axis_size("ctx")), "ctx", 0, 0), axis=0
+        ),
     )
     scale = 1.0 / DH**0.5
     query_heads = heads_split(queries)

time: 536 us -> 530 us (0.989)
  blocking collectives: 43.3 us -> 20.5 us
  starting transfers between devices: 10.7 us -> 18.1 us
  waiting for transfers between devices: 334 us -> 341 us
    all_gather x1 -> x0, blocking collectives: 22.8 us -> none  [per_device(): lax.all_gather(values_local, 'ctx', axis=0, tiled=True)]
    all_to_all x0 -> x1, starting transfers between devices: none -> 7.41 us  [per_device(): lax.all_to_all(jnp.stack([values_local] * lax.axis_size('ctx')), 'ctx', 0...]
    unnamed x42 -> x40, local copies, waits for them, and re-layouts: 35.3 us -> 35.3 us
  transfers between devices with their start and end apart: 7 -> 8, of which waited for: 3 -> 4; matrix products, arithmetic and copies ran while one was open for 14% -> 15% of each run, Pallas kernels for 0% -> 0%
where the time goes in v1:
time: 530 us; the launch traced here: 528 us
  waiting for transfers between devices  341 us (64%)
  local copies, waits for them, and re-layouts  73.9 us (14%)
  matrix products  48.6 us (9%)
  blocking collectives  20.5 us (4%)
  starting transfers between devices  18.1 us (3%)
  between operations  14.1 us (3%)
  other arithmetic  11.6 us (2%)
    unnamed x5, waiting for transfers between devices  237 us
    reduce_scatter x1, waiting for transfers between devices, per_device(): lax.psum_scatter(whole_terms, 'ctx', scatter_dimension=0, tiled=True)  99.7 us
    unnamed x40, local copies, waits for them, and re-layouts  35.3 us
    all_gather x1, blocking collectives, per_device(): lax.all_gather(keys_local, 'ctx', axis=0, tiled=True)  20.5 us
    dot_general x9, matrix products, dot_right_t(): lax.dot_general(left, right, (((1,), (1,)), ((), ())), preferred_element_...  18.7 us
    reshape x1, local copies, waits for them, and re-layouts, per_device(): (dot_left_t(windows, grad_rows) * factor).reshape(channels, kernel, chann...  14.8 us
  transfers between devices with their start and end apart: 8, of which 4 were waited for; matrix products, arithmetic and copies ran while one was open for 15% of the time, Pallas kernels for 0%

profile of v1, /device:TPU:8, one launch (start us, length us, event | category | flops | bytes accessed | tf_op | source)
XLA Modules:
  0.0 527.9 jit_solution(12977875594865591700)
XLA Ops:
  8.0 1.7 multiply_reduce_fusion.1
  10.3 1.9 collective-permute-start
  12.3 3.9 collective-permute-start.1
  16.2 2.5 fusion.22
  18.7 1.1 fusion.40
  22.3 1.1 bitcast_reduce_fusion
  23.4 0.9 fusion.39
  24.3 0.9 convolution_convert_fusion.2
  25.6 20.5 %all_gather.3 = bf16[512,768]{1,0:T(8,128)(2,1)} all-gather(bf16[32,768]{1,0:T(8,128)(2,1)S(1)} %convolution_convert_fusion.5), channel_id=1, replica_groups=mesh['dp'=16,'ctx'=16] {'ctx'}, dimensions={0}, use_global_device_ids=true | all-gather | bytes 835584 | tf_op jit(solution)/shard_map/all_gather | solution.py:85
  46.0 2.3 copy.33
  48.3 1.8 stack.14
  50.1 7.4 %all-to-all-start = ((bf16[16,32,768]{2,1,0:T(8,128)(2,1)}), bf16[16,32,768]{2,1,0:T(8,128)(2,1)}, u32[]{:S(2)}, u32[]{:S(2)}) async-start(bf16[16,32,768]{2,1,0:T(8,128)(2,1)} %stack.14), calls=%async_computation | async-start | bytes 1572864 | tf_op jit(solution)/shard_map/all_to_all | solution.py:87
  57.6 1.4 convolution_multiply_fusion.1
  60.6 2.8 fusion.79
  63.5 3.9 all-to-all-done
  67.4 2.7 reshape_reshape.3
  70.1 2.6 fusion.38
  72.7 1.9 fusion.32
  75.7 1.9 pad_maximum_fusion
  77.7 3.6 copy.48
  82.0 1.1 bitcast_dynamic-update-slice_fusion.4
  83.0 1.1 bitcast_dynamic-update-slice_fusion.3
  84.1 1.6 bitcast_dynamic-update-slice_fusion.2
  85.7 1.2 bitcast_dynamic-update-slice_fusion.1
  86.9 1.1 bitcast_dynamic-update-slice_fusion
  87.9 8.4 %copy.44 = bf16[512,768,5]{0,2,1:T(8,128)(2,1)} copy(bf16[512,768,5]{1,0,2:T(8,128)(2,1)} %bitcast_dynamic-update-slice_fusion) | data formatting | bytes 7864320 | tf_op jit(solution)/shard_map/stack | solution.py:146
  96.4 8.5 %reshape.80 = bf16[512,3840]{0,1:T(8,128)(2,1)} reshape(bf16[512,768,5]{0,2,1:T(8,128)(2,1)} %copy.44) | data formatting | bytes 7864320 | tf_op jit(solution)/shard_map/reshape | solution.py:148
  104.9 1.3 fusion.41
  106.2 1.3 convolution_add_fusion.2
  107.5 41.6 %reduce-scatter.10.cloned.1.call-done = f32[32,1536]{1,0:T(8,128)} async-done(((f32[512,1536]{1,0:T(8,128)}), f32[32,1536]{1,0:T(8,128)}) %reduce-scatter.10.cloned.1.call-update) | async-done | bytes 196624
  149.1 1.1 copy.49
  150.3 1.7 convolution_add_fusion.1
  152.6 9.7 %convolution_multiply_fusion = f32[3840,768]{1,0:T(8,128)} fusion(bf16[512,3840]{0,1:T(8,128)(2,1)} %reshape.80, bf16[512,768]{1,0:T(8,128)(2,1)S(1)} %bitcast.145), kind=kOutput, calls=%fused_computation.1 | convolution fusion | flops 3022848000 | bytes 16515072 | tf_op jit(solution)/shard_map/dot_general | solution.py:47
  162.3 14.8 %reshape.81 = f32[768,5,768]{2,1,0:T(8,128)} reshape(f32[3840,768]{1,0:T(8,128)} %convolution_multiply_fusion) | data formatting | bytes 23592960 | tf_op jit(solution)/shard_map/reshape | solution.py:150
  177.2 2.5 collective-permute-start.2
  179.7 3.2 fusion.20
  182.9 2.1 collective-permute-start.3
  185.1 3.2 fusion.24
  188.3 99.7 %reduce-scatter.8.cloned.1.call-done = f32[48,5,768]{2,1,0:T(8,128)} async-done(((f32[768,5,768]{2,1,0:T(8,128)}), f32[48,5,768]{2,1,0:T(8,128)}) %reduce-scatter.8.cloned.1.call-update) | async-done | bytes 737296 | tf_op jit(solution)/shard_map/reduce_scatter | solution.py:151
  288.0 13.1 %copy.50 = f32[48,5,768]{1,0,2:T(8,128)} copy(f32[48,5,768]{2,1,0:T(8,128)} %reduce-scatter.8.cloned.1.call-done) | data formatting | bytes 1474560
  301.1 12.9 %reshape.85 = f32[768,240]{1,0:T(8,128)} reshape(f32[768,48,5]{2,1,0:T(8,128)} %bitcast.139) | data formatting | bytes 1474560
  314.0 2.1 fusion.28
  316.2 2.2 fusion.16
  318.4 3.3 multiply_reduce_fusion
  321.7 1.3 fusion.60
  323.0 195.8 %reduce-scatter.12.cloned.1.call-done = f32[48,240]{1,0:T(8,128)} async-done(((f32[768,240]{1,0:T(8,128)}), f32[48,240]{1,0:T(8,128)}) %reduce-scatter.12.cloned.1.call-update) | async-done | bytes 46096
  518.8 1.4 reshape.86
  520.2 1.2 copy.45
  (58 shorter events, 8.4 us)
Async XLA Ops:
  7.2 16.2 %copy-start = (bf16[768,768]{1,0:T(8,128)(2,1)S(1)}, bf16[768,768]{1,0:T(8,128)(2,1)}, u32[]{:S(2)}) copy-start(bf16[768,768]{1,0:T(8,128)(2,1)} %param.15) | copy-start | bytes 3538948
  10.3 9.5 %collective-permute-start = (bf16[1,2,768]{2,1,0:T(2,128)(2,1)S(1)}, bf16[1,2,768]{2,1,0:T(2,128)(2,1)S(1)}, u32[]{:S(2)}, u32[]{:S(2)}) collective-permute-start(bf16[1,2,768]{2,1,0:T(2,128)(2,1)S(1)} %get-tuple-element.8), channel_id=1, source_target_pairs={{0,1},{1,2},{2,3},{3,4},{4,5},{5,6},{6,7},{7,8},{8,9},{9,10},{10,1... | collective-permute-start | bytes 9224 | tf_op jit(solution)/shard_map/ppermute | solution.py:18
  12.3 6.4 %copy-start.8 = (bf16[768,768]{1,0:T(8,128)(2,1)S(1)}, bf16[768,768]{1,0:T(8,128)(2,1)}, u32[]{:S(2)}) copy-start(bf16[768,768]{1,0:T(8,128)(2,1)} %param.18) | copy-start | bytes 3538948
  12.3 6.4 %copy-start.12 = (bf16[1,32,768]{2,1,0:T(8,128)(2,1)S(1)}, bf16[1,32,768]{2,1,0:T(8,128)(2,1)}, u32[]{:S(2)}) copy-start(bf16[1,32,768]{2,1,0:T(8,128)(2,1)} %param.19) | copy-start | bytes 147460
  12.3 7.5 %copy-start.11 = (bf16[5,768,768]{2,1,0:T(8,128)(2,1)S(1)}, bf16[5,768,768]{2,1,0:T(8,128)(2,1)}, u32[]{:S(2)}) copy-start(bf16[5,768,768]{2,1,0:T(8,128)(2,1)} %param.14) | copy-start | bytes 17694724
  12.3 9.2 %collective-permute-start.1 = (bf16[1,2,768]{2,1,0:T(2,128)(2,1)S(1)}, bf16[1,2,768]{2,1,0:T(2,128)(2,1)S(1)}, u32[]{:S(2)}, u32[]{:S(2)}) collective-permute-start(bf16[1,2,768]{2,1,0:T(2,128)(2,1)S(1)} %get-tuple-element.9), channel_id=1, source_target_pairs={{1,0},{2,1},{3,2},{4,3},{5,4},{6,5},{7,6},{8,7},{9,8},{10,9},{11,1... | collective-permute-start | bytes 9224 | tf_op jit(solution)/shard_map/ppermute | solution.py:21
  19.8 0.8 copy-start.13
  22.3 2.1 copy-start.5
  23.4 1.9 copy-start.4
  50.1 17.3 %all-to-all-start = ((bf16[16,32,768]{2,1,0:T(8,128)(2,1)}), bf16[16,32,768]{2,1,0:T(8,128)(2,1)}, u32[]{:S(2)}, u32[]{:S(2)}) async-start(bf16[16,32,768]{2,1,0:T(8,128)(2,1)} %stack.14), calls=%async_computation | async-start | bytes 1572864 | tf_op jit(solution)/shard_map/all_to_all | solution.py:87
  57.5 91.6 %reduce-scatter.10.cloned.1.call-start = ((), (), s32[]{:S(2)}) async-start(), calls=%async_computation.5 | async-start | bytes 3342336
  59.0 0.7 copy-start.7
  72.7 2.6 copy-start.10
  72.7 3.0 copy-start.3
  74.6 0.7 copy-start.9
  81.3 0.7 copy-start.14
  81.3 206.7 %reduce-scatter.8.cloned.1.call-start = ((), (), s32[]{:S(2)}) async-start(), calls=%async_computation.4 | async-start | bytes 20054016 | tf_op jit(solution)/shard_map/reduce_scatter | solution.py:151
  96.4 8.5 %copy-start.2 = (bf16[512,768]{0,1:T(8,128)(2,1)S(1)}, bf16[512,768]{0,1:T(8,128)(2,1)}, u32[]{:S(2)}) copy-start(bf16[512,768]{0,1:T(8,128)(2,1)} %copy.33) | copy-start | bytes 2359300
  107.5 44.6 %copy-start.6 = (bf16[768,768]{1,0:T(8,128)(2,1)S(1)}, bf16[768,768]{1,0:T(8,128)(2,1)}, u32[]{:S(2)}) copy-start(bf16[768,768]{1,0:T(8,128)(2,1)} %param.17) | copy-start | bytes 3538948
  177.2 341.7 %reduce-scatter.12.cloned.1.call-start = ((), (), s32[]{:S(2)}) async-start(), calls=%async_computation.6 | async-start | bytes 835584
  177.2 7.9 %collective-permute-start.2 = (bf16[1,2,768]{2,1,0:T(2,128)(2,1)S(1)}, bf16[1,2,768]{2,1,0:T(2,128)(2,1)S(1)}, u32[]{:S(2)}, u32[]{:S(2)}) collective-permute-start(bf16[1,2,768]{2,1,0:T(2,128)(2,1)S(1)} %get-tuple-element.6), channel_id=1, source_target_pairs={{1,0},{2,1},{3,2},{4,3},{5,4},{6,5},{7,6},{8,7},{9,8},{10,9},{11,1... | collective-permute-start | bytes 9224 | tf_op jit(solution)/shard_map/ppermute | solution.py:21
  182.9 133.2 %collective-permute-start.3 = (bf16[1,2,768]{2,1,0:T(2,128)(2,1)S(1)}, bf16[1,2,768]{2,1,0:T(2,128)(2,1)S(1)}, u32[]{:S(2)}, u32[]{:S(2)}) collective-permute-start(bf16[1,2,768]{2,1,0:T(2,128)(2,1)S(1)} %get-tuple-element.7), channel_id=1, source_target_pairs={{0,1},{1,2},{2,3},{3,4},{4,5},{5,6},{6,7},{7,8},{8,9},{9,10},{10,1... | collective-permute-start | bytes 9224 | tf_op jit(solution)/shard_map/ppermute | solution.py:18
  316.1 2.3 copy-start.15
  316.1 2.3 copy-start.16
  321.7 199.7 %copy-start.1 = (bf16[768,768]{1,0:T(8,128)(2,1)S(1)}, bf16[768,768]{1,0:T(8,128)(2,1)}, u32[]{:S(2)}) copy-start(bf16[768,768]{1,0:T(8,128)(2,1)} %param.15) | copy-start | bytes 3538948
Sparse Core Ops, SparseCore 0:
  81.4 67.6 reduce-scatter.9
  177.3 110.6 reduce-scatter.7
  314.1 204.6 reduce-scatter.11
